TPU v7x, 256 devices: a whole 4x4x8 slice. The times are simulated.
256 devices in a mesh: seq: 128 (over y, x_lo, z, core), mp: 2 (over x_hi).
Axes of the slice: x: 4 (x_hi: 2, x_lo: 2; x = x_hi * 2 + x_lo), y: 4, z: 8, core: 2. Of those that a mesh axis runs over, the one named last changes fastest.
Arguments:
- norm_gain: float32 [4096], P('mp'), may hold values from 0.25 to 1.75
- queries: bfloat16 [65536, 4096], P('seq', 'mp'), may hold values from -6 to 6
- keys: bfloat16 [65536, 4096], P('seq', 'mp'), may hold values from -6 to 6
- values: bfloat16 [65536, 4096], P('seq', 'mp'), may hold values from -6 to 6
Outputs:
- attended: bfloat16 [65536, 4096], P('seq', 'mp')
All inputs are finite; a program needn't handle non-finite values.
Results may differ from a plain program's by a relative error of at most 0.012.
Values may be sent and summed in bfloat16 or wider, within the bound.
A program may use at most 128 MiB of HBM per device.

v0:
```python
import functools
import math

import jax
import jax.numpy as jnp
from jax import lax
from jax.experimental import pallas as pl
from jax.experimental.pallas import tpu as pltpu
from jax.sharding import PartitionSpec as P

D = 4096
HEAD_DIM = 128
MESH = pl.DeviceIdType.MESH
SCALE = math.log2(math.e) / math.sqrt(HEAD_DIM)
EXCLUDED = -1e30

LEAD = 3
FORWARD_1, FORWARD_2, TASK_3, TASK_2, TASK_1, TASK_0 = 0, 1, 2, 3, 4, 5


def partial_attention(keys, values_t, queries, causal):
    scores = lax.dot_general(
        keys, queries, (((1,), (1,)), ((), ())), preferred_element_type=jnp.float32
    )
    if causal:
        rows, tile = scores.shape
        source = lax.broadcasted_iota(jnp.int32, (rows, tile), 0)
        target = lax.broadcasted_iota(jnp.int32, (rows, tile), 1) + (rows - tile)
        scores = jnp.where(source <= target, scores, EXCLUDED)
    top = jnp.max(scores, axis=0, keepdims=True) * SCALE
    weights = jnp.exp2(scores * SCALE - top)
    total = jnp.sum(weights, axis=0, keepdims=True)
    output = lax.dot_general(
        values_t,
        weights.astype(jnp.bfloat16),
        (((1,), (0,)), ((), ())),
        preferred_element_type=jnp.float32,
    )
    return output, top, total


def kernel(
    n, heads, rows,
    gain_ref, q_hbm, k_hbm, v_hbm, out_hbm,
    q_own, k_own, v_own, v_t, q_in, o_in, l_in, o_out, l_out, attended, finished,
    squares, squares_in,
    load_sem, q_send, q_recv, o_send, o_recv, l_send, l_recv, s_send, s_recv, out_sem,
):
    me = lax.axis_index("seq")
    partner = 1 - lax.axis_index("mp")
    left, right = jnp.maximum(me - 1, 0), jnp.minimum(me + 1, n - 1)
    has_left, has_right = me > 0, me < n - 1
    half = rows // 2
    to_left, to_right = {"seq": left}, {"seq": right}

    def columns(h):
        return pl.ds(pl.multiple_of(h * HEAD_DIM, HEAD_DIM), HEAD_DIM)

    def load(which, h):
        source, target = ((q_hbm, q_own), (k_hbm, k_own), (v_hbm, v_own))[which]
        return pltpu.make_async_copy(
            source.at[:, columns(h)], target.at[h], load_sem.at[which, h]
        )

    def send_q(step, h):
        source = q_hbm.at[:, columns(h)] if step == 0 else q_in.at[step - 1, h]
        return pltpu.make_async_remote_copy(
            src_ref=source, dst_ref=q_in.at[step, h],
            send_sem=q_send.at[step, h], recv_sem=q_recv.at[step, h],
            device_id=to_left, device_id_type=MESH,
        )

    def send_o(step, h):
        return pltpu.make_async_remote_copy(
            src_ref=o_out.at[step, h], dst_ref=o_in.at[step, h],
            send_sem=o_send.at[step, h], recv_sem=o_recv.at[step, h],
            device_id=to_right, device_id_type=MESH,
        )

    def send_l(step, h):
        return pltpu.make_async_remote_copy(
            src_ref=l_out.at[step, h], dst_ref=l_in.at[step, h],
            send_sem=l_send.at[step, h], recv_sem=l_recv.at[step, h],
            device_id=to_right, device_id_type=MESH,
        )

    def send_s():
        return pltpu.make_async_remote_copy(
            src_ref=squares, dst_ref=squares_in, send_sem=s_send, recv_sem=s_recv,
            device_id={"mp": partner}, device_id_type=MESH,
        )

    barrier = pltpu.get_barrier_semaphore()

    @pl.when(has_left)
    def _():
        pl.semaphore_signal(barrier, inc=1, device_id=to_left, device_id_type=MESH)

    @pl.when(has_right)
    def _():
        pl.semaphore_signal(barrier, inc=1, device_id=to_right, device_id_type=MESH)

    pl.semaphore_signal(barrier, inc=1, device_id={"mp": partner}, device_id_type=MESH)

    @pl.loop(0, heads)
    def _(h):
        for which in range(3):
            load(which, h).start()

    squares[...] = jnp.zeros_like(squares)

    @pl.when(jnp.logical_not(has_left))
    def _():
        @pl.loop(0, heads)
        def _(h):
            for step in range(3):
                o_in[step, h] = jnp.zeros(o_in.shape[2:], o_in.dtype)
                l_in[step, h] = jnp.full(l_in.shape[2:], EXCLUDED, l_in.dtype)

    pl.semaphore_wait(
        barrier, 1 + has_left.astype(jnp.int32) + has_right.astype(jnp.int32)
    )

    @pl.when(has_left)
    def _():
        for h in range(min(LEAD, heads)):
            send_q(0, h).start()

    def staged(r, skew, distance, run):
        h = r - skew
        @pl.when((h >= 0) & (h < heads) & (me + distance < n))
        def _():
            run(h)

    def prepare(h):
        for which in range(3):
            load(which, h).wait()
        v_t[h] = v_own[h].T

    def forward(step, h):
        send_q(step - 1, h).wait_recv()

        @pl.when(has_left)
        def _():
            send_q(step, h).start()

    def task(distance, h):
        causal = distance == 0
        if distance:
            queries = q_in.at[distance - 1, h]
        else:
            queries = q_own.at[h]
        if distance == 3:
            send_q(2, h).wait_recv()
        parts = []
        for at in range(0, rows, half):
            depth = at + half if causal else rows
            parts.append(
                partial_attention(
                    k_own[h, :depth], v_t[h, :, :depth], queries[at : at + half], causal
                )
            )
        if distance < 3:
            @pl.when(has_left)
            def _():
                send_o(2 - distance, h).wait_recv()
                send_l(2 - distance, h).wait_recv()

        for at, (output, top, total) in zip(range(0, rows, half), parts):
            span = slice(at, at + half)
            if distance == 3:
                mixed = output / total
                level = top + jnp.log2(total)
            else:
                before = l_in[2 - distance, h, :, span]
                high = jnp.maximum(before, top)
                weight_before = jnp.exp2(before - high)
                weight_here = jnp.exp2(top - high)
                whole = weight_before + weight_here * total
                mixed = (
                    o_in[2 - distance, h, :, span].astype(jnp.float32) * (weight_before / whole)
                    + output * (weight_here / whole)
                )
                level = high + jnp.log2(whole)
            if distance:
                o_out[3 - distance, h, :, span] = mixed.astype(jnp.bfloat16)
                l_out[3 - distance, h, :, span] = level
            else:
                attended[h, span] = mixed.T
                squares[:, span] += jnp.sum(mixed * mixed, axis=0, keepdims=True)
        if distance:
            send_o(3 - distance, h).start()
            send_l(3 - distance, h).start()

    @pl.loop(0, heads + TASK_0)
    def _(r):
        @pl.when(has_left & (r + LEAD < heads))
        def _():
            send_q(0, r + LEAD).start()

        staged(r, 0, 0, prepare)
        staged(r, FORWARD_1, 1, functools.partial(forward, 1))
        staged(r, FORWARD_2, 2, functools.partial(forward, 2))
        staged(r, TASK_3, 3, functools.partial(task, 3))
        staged(r, TASK_2, 2, functools.partial(task, 2))
        staged(r, TASK_1, 1, functools.partial(task, 1))
        staged(r, TASK_0, 0, functools.partial(task, 0))

    send_s().start()
    send_s().wait()
    scale = lax.rsqrt((squares[...] + squares_in[...]) / D + 1e-06)
    scale = jnp.broadcast_to(scale, (HEAD_DIM, rows)).T

    def store(h):
        return pltpu.make_async_copy(finished.at[h], out_hbm.at[:, columns(h)], out_sem.at[h])

    @pl.loop(0, heads)
    def _(h):
        gain = gain_ref[h]
        finished[h] = (attended[h] * scale * gain).astype(jnp.bfloat16)
        store(h).start()

    @pl.loop(0, heads)
    def _(h):
        store(h).wait()
        for step in range(3):
            @pl.when(has_left & (me + step < n))
            def _():
                send_q(step, h).wait_send()

            @pl.when(me + 3 - step < n)
            def _():
                send_o(step, h).wait_send()
                send_l(step, h).wait_send()


def solution(mesh):
    n = mesh.shape["seq"]

    def shards(norm_gain, queries, keys, values):
        rows, width = queries.shape
        heads = width // HEAD_DIM
        by_head = (heads, rows, HEAD_DIM)
        turned = (heads, HEAD_DIM, rows)
        dma = pltpu.SemaphoreType.DMA
        gain = norm_gain.reshape(heads, 1, HEAD_DIM)
        return pl.pallas_call(
            functools.partial(kernel, n, heads, rows),
            out_shape=jax.ShapeDtypeStruct(queries.shape, jnp.bfloat16),
            in_specs=[pl.BlockSpec(memory_space=pltpu.VMEM)]
            + [pl.BlockSpec(memory_space=pl.ANY)] * 3,
            out_specs=pl.BlockSpec(memory_space=pl.ANY),
            scratch_shapes=[
                pltpu.VMEM(by_head, jnp.bfloat16),
                pltpu.VMEM(by_head, jnp.bfloat16),
                pltpu.VMEM(by_head, jnp.bfloat16),
                pltpu.VMEM(turned, jnp.bfloat16),
                pltpu.VMEM((3, *by_head), jnp.bfloat16),
                pltpu.VMEM((3, *turned), jnp.bfloat16),
                pltpu.VMEM((3, heads, 1, rows), jnp.float32),
                pltpu.VMEM((3, *turned), jnp.bfloat16),
                pltpu.VMEM((3, heads, 1, rows), jnp.float32),
                pltpu.VMEM(by_head, jnp.float32),
                pltpu.VMEM(by_head, jnp.bfloat16),
                pltpu.VMEM((1, rows), jnp.float32),
                pltpu.VMEM((1, rows), jnp.float32),
                dma((3, heads)),
                dma((3, heads)),
                dma((3, heads)),
                dma((3, heads)),
                dma((3, heads)),
                dma((3, heads)),
                dma((3, heads)),
                dma,
                dma,
                dma((heads,)),
            ],
            compiler_params=pltpu.CompilerParams(
                collective_id=0, has_side_effects=True, vmem_limit_bytes=56 << 20
            ),
            cost_estimate=pl.CostEstimate(
                flops=16 * heads * rows * rows * HEAD_DIM,
                bytes_accessed=8 * rows * width,
                transcendentals=4 * heads * rows * rows,
            ),
        )(gain, queries, keys, values)

    placed = (P("mp"), P("seq", "mp"), P("seq", "mp"), P("seq", "mp"))
    return jax.shard_map(
        shards, mesh=mesh, in_specs=placed, out_specs=P("seq", "mp"), check_vma=False
    )
```

profile of v0, /device:TPU:24, one launch (start us, length us, event | category | flops | bytes accessed | tf_op | source)
XLA Modules:
  0.0 127.6 jit_solution(12076752431909040212)
XLA Ops:
  0.0 124.5 %shard_map.46 = bf16[512,2048]{1,0:T(8,128)(2,1)} custom-call(f32[16,1,128]{2,1,0:T(1,128)} %bitcast.1, bf16[512,2048]{1,0:T(8,128)(2,1)} %q_hbm.1, bf16[512,2048]{1,0:T(8,128)(2,1)} %k_hbm.1, bf16[512,2048]{1,0:T(8,128)(2,1)} %v_hbm.1), custom_call_target="tpu_custom_call" | custom-call | flops 8589934592 | bytes 8388608 | tf_op jit(solution)/shard_map/pallas_call | solution.py:247
  124.5 3.2 %copy.6 = bf16[512,2048]{1,0:T(8,128)(2,1)} copy(bf16[512,2048]{1,0:T(8,128)(2,1)} %shard_map.46) | data formatting | bytes 4194304
where the time goes:
time: 128 us
  Pallas kernels  124 us (97%)
  local copies, waits for them, and re-layouts  3.16 us (2%)
    pallas_call x1, Pallas kernels, shards(): pl.pallas_call(functools.partial(kernel, n, heads, rows), out_shape=jax.S...  124 us
    unnamed x1, local copies, waits for them, and re-layouts  3.16 us

commit v1 on v0

v1 whole, which is shorter than its diff:
```python
import functools
import math

import jax
import jax.numpy as jnp
from jax import lax
from jax.experimental import pallas as pl
from jax.experimental.pallas import tpu as pltpu
from jax.sharding import PartitionSpec as P

D = 4096
HEAD_DIM = 128
MESH = pl.DeviceIdType.MESH
SCALE = math.log2(math.e) / math.sqrt(HEAD_DIM)
EXCLUDED = -1e30

SHIPPED = 2
LEAD = 2
FORWARD_1, FORWARD_2, ATTEND, MERGE_2, MERGE_1, MERGE_0 = (1, 3), (1, 5), (4, 6), (6, 7), (7, 8), (10, 12)
SHIP_1, SHIP_2, ATTEND_SHIPPED = (2, 2), (4, 5), (6, 7)
SLOTS = max(b - a for a, b in zip(ATTEND, MERGE_0)) + 1
TILE = 128


def across(a, b):
    return lax.dot_general(a, b, (((1,), (1,)), ((), ())), preferred_element_type=jnp.float32)


def lanes_to_row(column):
    return column.T[:1]


def row_to_lanes(row):
    return jnp.broadcast_to(row, (HEAD_DIM, row.shape[1])).T


def kernel(
    n, heads, kept, rows,
    gain_ref, q_hbm, k_hbm, v_hbm, out_hbm,
    q_own, k_own, v_own, q_in, o_in, l_in, o_out, l_out, o_own, l_own, k_in, v_in, attended, finished,
    squares, row_out, row_in,
    load_sem, q_send, q_recv, o_send, o_recv, l_send, l_recv, kv_send, kv_recv, s_send, s_recv, out_sem,
):
    me = lax.axis_index("seq")
    partner = 1 - lax.axis_index("mp")
    left, right = jnp.maximum(me - 1, 0), jnp.minimum(me + 1, n - 1)
    has_left, has_right = me > 0, me < n - 1
    tile = min(TILE, rows)
    to_left, to_right = {"seq": left}, {"seq": right}

    def columns(h):
        return pl.ds(pl.multiple_of(h * HEAD_DIM, HEAD_DIM), HEAD_DIM)

    def load(which, h):
        source, target = ((q_hbm, q_own), (k_hbm, k_own), (v_hbm, v_own))[which]
        return pltpu.make_async_copy(
            source.at[:, columns(h)], target.at[h], load_sem.at[which, h]
        )

    def send_q(step, h):
        source = q_hbm.at[:, columns(h)] if step == 0 else q_in.at[step - 1, h]
        return pltpu.make_async_remote_copy(
            src_ref=source, dst_ref=q_in.at[step, h],
            send_sem=q_send.at[step, h], recv_sem=q_recv.at[step, h],
            device_id=to_left, device_id_type=MESH,
        )

    def send_o(step, h):
        return pltpu.make_async_remote_copy(
            src_ref=o_out.at[step, h], dst_ref=o_in.at[step, h],
            send_sem=o_send.at[step, h], recv_sem=o_recv.at[step, h],
            device_id=to_right, device_id_type=MESH,
        )

    def send_l(step, h):
        return pltpu.make_async_remote_copy(
            src_ref=l_out.at[step, h], dst_ref=l_in.at[step, h],
            send_sem=l_send.at[step, h], recv_sem=l_recv.at[step, h],
            device_id=to_right, device_id_type=MESH,
        )

    def send_kv(which, step, j):
        source, target = ((k_hbm, k_in), (v_hbm, v_in))[which]
        source = target.at[step - 1, j] if step else source.at[:, columns(kept + j)]
        return pltpu.make_async_remote_copy(
            src_ref=source, dst_ref=target.at[step, j],
            send_sem=kv_send.at[which, step, j], recv_sem=kv_recv.at[which, step, j],
            device_id=to_right, device_id_type=MESH,
        )

    def send_s():
        return pltpu.make_async_remote_copy(
            src_ref=row_out, dst_ref=row_in, send_sem=s_send, recv_sem=s_recv,
            device_id={"mp": partner}, device_id_type=MESH,
        )

    barrier = pltpu.get_barrier_semaphore()

    @pl.when(has_left)
    def _():
        pl.semaphore_signal(barrier, inc=1, device_id=to_left, device_id_type=MESH)

    @pl.when(has_right)
    def _():
        pl.semaphore_signal(barrier, inc=1, device_id=to_right, device_id_type=MESH)

    pl.semaphore_signal(barrier, inc=1, device_id={"mp": partner}, device_id_type=MESH)

    @pl.loop(0, heads)
    def _(h):
        for which in range(3):
            load(which, h).start()

    squares[...] = jnp.zeros_like(squares)

    @pl.when(jnp.logical_not(has_left))
    def _():
        @pl.loop(0, kept)
        def _(h):
            for step in range(3):
                o_in[step, h] = jnp.zeros(o_in.shape[2:], o_in.dtype)
                l_in[step, h] = jnp.full(l_in.shape[2:], EXCLUDED, l_in.dtype)

    for step in range(3):
        @pl.when(me <= step)
        def _():
            for j in range(heads - kept):
                k_in[step, j] = jnp.zeros(k_in.shape[2:], k_in.dtype)
                v_in[step, j] = jnp.zeros(v_in.shape[2:], v_in.dtype)

    pl.semaphore_wait(
        barrier, 1 + has_left.astype(jnp.int32) + has_right.astype(jnp.int32)
    )

    @pl.when(has_right)
    def _():
        for j in range(heads - kept):
            for which in range(2):
                send_kv(which, 0, j).start()

    @pl.when(has_left)
    def _():
        for h in range(min(LEAD, kept)):
            send_q(0, h).start()

    def rounds(skew):
        return skew[0] + lax.rem(me, 2) * (skew[1] - skew[0])

    def staged(r, skew, distance, run):
        h = r - rounds(skew)
        @pl.when((h >= 0) & (h < kept) & (me + distance < n))
        def _():
            run(h)

    def staged_shipped(r, skew, run):
        j = r - rounds(skew)
        @pl.when((j >= 0) & (j < heads - kept))
        def _():
            run(j)

    def ship(step, j):
        @pl.when(me >= step)
        def _():
            for which in range(2):
                send_kv(which, step - 1, j).wait_recv()

                @pl.when(has_right)
                def _():
                    send_kv(which, step, j).start()

    def attend_shipped(j):
        h = kept + j
        for which in range(3):
            load(which, h).wait()

        @pl.when(me >= 3)
        def _():
            for which in range(2):
                send_kv(which, 2, j).wait_recv()

        ones = jnp.ones((rows, HEAD_DIM), jnp.bfloat16)
        for at in range(0, rows, tile):
            span = slice(at, at + tile)
            queries = q_own[h, span]
            parts = [causal(across(queries, k_own[h, : at + tile]), at)]
            for step in range(3):
                scores = across(queries, k_in[step, j])
                parts.append(jnp.where(me > step, scores, EXCLUDED))
            top = functools.reduce(
                jnp.maximum, [jnp.max(part, axis=1, keepdims=True) for part in parts]
            )
            both = jnp.zeros((tile, 2 * HEAD_DIM), jnp.float32)
            for step, scores in enumerate(parts):
                weights = jnp.exp2(scores * SCALE - top * SCALE).astype(jnp.bfloat16)
                values = v_in[step - 1, j] if step else v_own[h, : at + tile]
                values = jnp.concatenate([values, ones[: values.shape[0]]], 1)
                both += jnp.dot(weights, values, preferred_element_type=jnp.float32)
            mixed = both[:, :HEAD_DIM] / both[:, HEAD_DIM:]
            attended[h, span] = mixed
            squares[span] += mixed * mixed

    def causal(scores, at):
        target = lax.broadcasted_iota(jnp.int32, scores.shape, 0) + at
        source = lax.broadcasted_iota(jnp.int32, scores.shape, 1)
        return jnp.where(source <= target, scores, EXCLUDED)

    def forward(step, h):
        send_q(step - 1, h).wait_recv()

        @pl.when(has_left)
        def _():
            send_q(step, h).start()

    def attend(h):
        for which in range(3):
            load(which, h).wait()

        @pl.when(me + 3 < n)
        def _():
            send_q(2, h).wait_recv()

        slot = lax.rem(h, SLOTS)
        keys = k_own[h]
        values = jnp.concatenate([v_own[h], jnp.ones((rows, HEAD_DIM), jnp.bfloat16)], 1)
        lane = lax.broadcasted_iota(jnp.int32, (tile, HEAD_DIM), 1)
        for at in range(0, rows, tile):
            span = slice(at, at + tile)
            levels = jnp.zeros((tile, HEAD_DIM), jnp.float32)
            for distance in (3, 2, 1, 0):
                depth = rows if distance else at + tile
                queries = q_in[distance - 1, h, span] if distance else q_own[h, span]
                scores = across(queries, keys[:depth])
                if not distance:
                    scores = causal(scores, at)
                top = jnp.max(scores, axis=1, keepdims=True) * SCALE
                weights = jnp.exp2(scores * SCALE - top).astype(jnp.bfloat16)
                both = jnp.dot(weights, values[:depth], preferred_element_type=jnp.float32)
                total = both[:, HEAD_DIM:]
                output = both[:, :HEAD_DIM] * (1.0 / total)
                levels = jnp.where(lane == distance, top + jnp.log2(total), levels)
                if distance == 3:
                    o_out[0, h, span] = output.astype(jnp.bfloat16)
                else:
                    o_own[slot, distance, span] = output
            turned = levels.T
            l_out[0, h, :, span] = turned[3:4]
            l_own[slot, :, span] = turned[:4]

        @pl.when(me + 3 < n)
        def _():
            send_o(0, h).start()
            send_l(0, h).start()

    def merge(distance, h):
        step = 3 - distance

        @pl.when(has_left)
        def _():
            send_o(step - 1, h).wait_recv()
            send_l(step - 1, h).wait_recv()

        slot = lax.rem(h, SLOTS)
        here, before = l_own[slot, distance : distance + 1], l_in[step - 1, h]
        share = 1.0 / (1.0 + jnp.exp2(here - before))
        if distance:
            gap = -jnp.abs(here - before)
            l_out[step, h] = jnp.maximum(here, before) + jnp.log2(1.0 + jnp.exp2(gap))
        share = row_to_lanes(share)
        mine = o_own[slot, distance]
        mixed = mine + share * (o_in[step - 1, h].astype(jnp.float32) - mine)
        if distance:
            o_out[step, h] = mixed.astype(jnp.bfloat16)
            send_o(step, h).start()
            send_l(step, h).start()
        else:
            attended[h] = mixed
            squares[...] += mixed * mixed

    @pl.loop(0, kept + max(MERGE_0))
    def _(r):
        staged_shipped(r, SHIP_1, functools.partial(ship, 1))
        staged_shipped(r, SHIP_2, functools.partial(ship, 2))
        staged_shipped(r, ATTEND_SHIPPED, attend_shipped)
        staged(r, FORWARD_1, 1, functools.partial(forward, 1))
        staged(r, MERGE_0, 0, functools.partial(merge, 0))

        @pl.when(has_left & (r + LEAD < kept))
        def _():
            send_q(0, r + LEAD).start()

        staged(r, MERGE_2, 2, functools.partial(merge, 2))
        staged(r, ATTEND, 0, attend)
        staged(r, FORWARD_2, 2, functools.partial(forward, 2))
        staged(r, MERGE_1, 1, functools.partial(merge, 1))

    row_out[...] = lanes_to_row(
        jnp.broadcast_to(jnp.sum(squares[...], axis=1, keepdims=True), squares.shape)
    )
    send_s().start()
    send_s().wait()
    scale = row_to_lanes(lax.rsqrt((row_out[...] + row_in[...]) / D + 1e-06))

    def store(h):
        return pltpu.make_async_copy(finished.at[h], out_hbm.at[:, columns(h)], out_sem.at[h])

    @pl.loop(0, heads)
    def _(h):
        gain = gain_ref[h]
        finished[h] = (attended[h] * scale * gain).astype(jnp.bfloat16)
        store(h).start()

    @pl.loop(0, heads)
    def _(h):
        store(h).wait()

    @pl.loop(0, kept)
    def _(h):
        for step in range(3):
            @pl.when(has_left & (me + step < n))
            def _():
                send_q(step, h).wait_send()

            @pl.when(me + 3 - step < n)
            def _():
                send_o(step, h).wait_send()
                send_l(step, h).wait_send()

    for step in range(3):
        @pl.when(has_right & (me >= step))
        def _():
            for j in range(heads - kept):
                for which in range(2):
                    send_kv(which, step, j).wait_send()


def solution(mesh):
    n = mesh.shape["seq"]

    def shards(norm_gain, queries, keys, values):
        rows, width = queries.shape
        heads = width // HEAD_DIM
        kept = heads - SHIPPED
        by_head = (heads, rows, HEAD_DIM)
        moved = (3, kept, rows, HEAD_DIM)
        shipped = (3, SHIPPED, rows, HEAD_DIM)
        dma = pltpu.SemaphoreType.DMA
        gain = norm_gain.reshape(heads, 1, HEAD_DIM)
        return pl.pallas_call(
            functools.partial(kernel, n, heads, kept, rows),
            out_shape=jax.ShapeDtypeStruct(queries.shape, jnp.bfloat16),
            in_specs=[pl.BlockSpec(memory_space=pltpu.VMEM)]
            + [pl.BlockSpec(memory_space=pl.ANY)] * 3,
            out_specs=pl.BlockSpec(memory_space=pl.ANY),
            scratch_shapes=[
                pltpu.VMEM(by_head, jnp.bfloat16),
                pltpu.VMEM(by_head, jnp.bfloat16),
                pltpu.VMEM(by_head, jnp.bfloat16),
                pltpu.VMEM(moved, jnp.bfloat16),
                pltpu.VMEM(moved, jnp.bfloat16),
                pltpu.VMEM((3, kept, 1, rows), jnp.float32),
                pltpu.VMEM(moved, jnp.bfloat16),
                pltpu.VMEM((3, kept, 1, rows), jnp.float32),
                pltpu.VMEM((SLOTS, 3, rows, HEAD_DIM), jnp.float32),
                pltpu.VMEM((SLOTS, 4, rows), jnp.float32),
                pltpu.VMEM(shipped, jnp.bfloat16),
                pltpu.VMEM(shipped, jnp.bfloat16),
                pltpu.VMEM(by_head, jnp.float32),
                pltpu.VMEM(by_head, jnp.bfloat16),
                pltpu.VMEM((rows, HEAD_DIM), jnp.float32),
                pltpu.VMEM((1, rows), jnp.float32),
                pltpu.VMEM((1, rows), jnp.float32),
                dma((3, heads)),
                dma((3, kept)),
                dma((3, kept)),
                dma((3, kept)),
                dma((3, kept)),
                dma((3, kept)),
                dma((3, kept)),
                dma((2, 3, SHIPPED)),
                dma((2, 3, SHIPPED)),
                dma,
                dma,
                dma((heads,)),
            ],
            compiler_params=pltpu.CompilerParams(
                collective_id=0, has_side_effects=True, vmem_limit_bytes=56 << 20
            ),
            cost_estimate=pl.CostEstimate(
                flops=16 * heads * rows * rows * HEAD_DIM,
                bytes_accessed=8 * rows * width,
                transcendentals=4 * heads * rows * rows,
            ),
        )(gain, queries, keys, values)

    placed = (P("mp"), P("seq", "mp"), P("seq", "mp"), P("seq", "mp"))
    return jax.shard_map(
        shards, mesh=mesh, in_specs=placed, out_specs=P("seq", "mp"), check_vma=False
    )
```

time: 128 us -> 101 us (0.79)
  Pallas kernels: 124 us -> 97.4 us
    pallas_call x1, Pallas kernels: 124 us -> 97.4 us  [shards(): pl.pallas_call(functools.partial(kernel, n, heads, kept, rows), out_shape...]
where the time goes in v1:
time: 101 us
  Pallas kernels  97.4 us (96%)
  local copies, waits for them, and re-layouts  3.16 us (3%)
    pallas_call x1, Pallas kernels, shards(): pl.pallas_call(functools.partial(kernel, n, heads, kept, rows), out_shape...  97.4 us
    unnamed x1, local copies, waits for them, and re-layouts  3.16 us

profile of v1, /device:TPU:24, one launch (start us, length us, event | category | flops | bytes accessed | tf_op | source)
XLA Modules:
  0.0 100.6 jit_solution(10643926988956093488)
XLA Ops:
  0.0 97.4 %shard_map.46 = bf16[512,2048]{1,0:T(8,128)(2,1)} custom-call(f32[16,1,128]{2,1,0:T(1,128)} %bitcast.1, bf16[512,2048]{1,0:T(8,128)(2,1)} %q_hbm.1, bf16[512,2048]{1,0:T(8,128)(2,1)} %k_hbm.1, bf16[512,2048]{1,0:T(8,128)(2,1)} %v_hbm.1), custom_call_target="tpu_custom_call" | custom-call | flops 8589934592 | bytes 8388608 | tf_op jit(solution)/shard_map/pallas_call | solution.py:348
  97.4 3.2 %copy.6 = bf16[512,2048]{1,0:T(8,128)(2,1)} copy(bf16[512,2048]{1,0:T(8,128)(2,1)} %shard_map.46) | data formatting | bytes 4194304

commit v2 on v1

--- a/solution.py
+++ b/solution.py
@@ -36,10 +36,10 @@
 
 def kernel(
     n, heads, kept, rows,
-    gain_ref, q_hbm, k_hbm, v_hbm, out_hbm,
-    q_own, k_own, v_own, q_in, o_in, l_in, o_out, l_out, o_own, l_own, k_in, v_in, attended, finished,
+    q_hbm, k_hbm, v_hbm, attended, scale_ref,
+    q_own, k_own, v_own, q_in, o_in, l_in, o_out, l_out, o_own, l_own, k_in, v_in,
     squares, row_out, row_in,
-    load_sem, q_send, q_recv, o_send, o_recv, l_send, l_recv, kv_send, kv_recv, s_send, s_recv, out_sem,
+    load_sem, q_send, q_recv, o_send, o_recv, l_send, l_recv, kv_send, kv_recv, s_send, s_recv,
 ):
     me = lax.axis_index("seq")
     partner = 1 - lax.axis_index("mp")
@@ -61,21 +61,21 @@
         source = q_hbm.at[:, columns(h)] if step == 0 else q_in.at[step - 1, h]
         return pltpu.make_async_remote_copy(
             src_ref=source, dst_ref=q_in.at[step, h],
-            send_sem=q_send.at[step, h], recv_sem=q_recv.at[step, h],
+            send_sem=q_send.at[step], recv_sem=q_recv.at[step, h],
             device_id=to_left, device_id_type=MESH,
         )
 
     def send_o(step, h):
         return pltpu.make_async_remote_copy(
             src_ref=o_out.at[step, h], dst_ref=o_in.at[step, h],
-            send_sem=o_send.at[step, h], recv_sem=o_recv.at[step, h],
+            send_sem=o_send.at[step], recv_sem=o_recv.at[step, h],
             device_id=to_right, device_id_type=MESH,
         )
 
     def send_l(step, h):
         return pltpu.make_async_remote_copy(
             src_ref=l_out.at[step, h], dst_ref=l_in.at[step, h],
-            send_sem=l_send.at[step, h], recv_sem=l_recv.at[step, h],
+            send_sem=l_send.at[step], recv_sem=l_recv.at[step, h],
             device_id=to_right, device_id_type=MESH,
         )
 
@@ -84,7 +84,7 @@
         source = target.at[step - 1, j] if step else source.at[:, columns(kept + j)]
         return pltpu.make_async_remote_copy(
             src_ref=source, dst_ref=target.at[step, j],
-            send_sem=kv_send.at[which, step, j], recv_sem=kv_recv.at[which, step, j],
+            send_sem=kv_send.at[which, step], recv_sem=kv_recv.at[which, step, j],
             device_id=to_right, device_id_type=MESH,
         )
 
@@ -297,40 +297,46 @@
         jnp.broadcast_to(jnp.sum(squares[...], axis=1, keepdims=True), squares.shape)
     )
     send_s().start()
+
+    def drain(buffer, sem):
+        pltpu.make_async_copy(buffer, buffer, sem).wait()
+
+    for step in range(3):
+        @pl.when(has_left & (me + step < n))
+        def _():
+            drain(q_in.at[step], q_send.at[step])
+
+        @pl.when(me + 3 - step < n)
+        def _():
+            drain(o_out.at[step], o_send.at[step])
+            drain(l_out.at[step], l_send.at[step])
+
+        @pl.when(has_right & (me >= step))
+        def _():
+            drain(k_in.at[step], kv_send.at[0, step])
+            drain(v_in.at[step], kv_send.at[1, step])
+
     send_s().wait()
-    scale = row_to_lanes(lax.rsqrt((row_out[...] + row_in[...]) / D + 1e-06))
-
-    def store(h):
-        return pltpu.make_async_copy(finished.at[h], out_hbm.at[:, columns(h)], out_sem.at[h])
-
-    @pl.loop(0, heads)
-    def _(h):
-        gain = gain_ref[h]
-        finished[h] = (attended[h] * scale * gain).astype(jnp.bfloat16)
-        store(h).start()
-
-    @pl.loop(0, heads)
-    def _(h):
-        store(h).wait()
-
-    @pl.loop(0, kept)
-    def _(h):
-        for step in range(3):
-            @pl.when(has_left & (me + step < n))
-            def _():
-                send_q(step, h).wait_send()
-
-            @pl.when(me + 3 - step < n)
-            def _():
-                send_o(step, h).wait_send()
-                send_l(step, h).wait_send()
-
-    for step in range(3):
-        @pl.when(has_right & (me >= step))
-        def _():
-            for j in range(heads - kept):
-                for which in range(2):
-                    send_kv(which, step, j).wait_send()
+    scale_ref[...] = row_to_lanes(lax.rsqrt((row_out[...] + row_in[...]) / D + 1e-06))
+
+
+def finish(gain_ref, attended, scale_ref, out_hbm, finished, sem):
+    heads, rows, _ = attended.shape
+    chunk = rows // 4
+
+    def store(i):
+        span = pl.ds(i * chunk, chunk)
+        return pltpu.make_async_copy(finished.at[span], out_hbm.at[span], sem.at[i])
+
+    for i in range(4):
+        span = slice(i * chunk, (i + 1) * chunk)
+        for h in range(heads):
+            columns = slice(h * HEAD_DIM, (h + 1) * HEAD_DIM)
+            scaled = attended[h, span] * scale_ref[span] * gain_ref[h]
+            finished[span, columns] = scaled.astype(jnp.bfloat16)
+        store(i).start()
+    for i in range(4):
+        store(i).wait()
 
 
 def solution(mesh):
@@ -345,12 +351,15 @@
         shipped = (3, SHIPPED, rows, HEAD_DIM)
         dma = pltpu.SemaphoreType.DMA
         gain = norm_gain.reshape(heads, 1, HEAD_DIM)
-        return pl.pallas_call(
+        whole = pl.BlockSpec(memory_space=pltpu.VMEM)
+        attended, scale = pl.pallas_call(
             functools.partial(kernel, n, heads, kept, rows),
-            out_shape=jax.ShapeDtypeStruct(queries.shape, jnp.bfloat16),
-            in_specs=[pl.BlockSpec(memory_space=pltpu.VMEM)]
-            + [pl.BlockSpec(memory_space=pl.ANY)] * 3,
-            out_specs=pl.BlockSpec(memory_space=pl.ANY),
+            out_shape=[
+                pltpu.VMEM(by_head, jnp.float32),
+                pltpu.VMEM((rows, HEAD_DIM), jnp.float32),
+            ],
+            in_specs=[pl.BlockSpec(memory_space=pl.ANY)] * 3,
+            out_specs=[whole, whole],
             scratch_shapes=[
                 pltpu.VMEM(by_head, jnp.bfloat16),
                 pltpu.VMEM(by_head, jnp.bfloat16),
@@ -364,23 +373,20 @@
                 pltpu.VMEM((SLOTS, 4, rows), jnp.float32),
                 pltpu.VMEM(shipped, jnp.bfloat16),
                 pltpu.VMEM(shipped, jnp.bfloat16),
-                pltpu.VMEM(by_head, jnp.float32),
-                pltpu.VMEM(by_head, jnp.bfloat16),
                 pltpu.VMEM((rows, HEAD_DIM), jnp.float32),
                 pltpu.VMEM((1, rows), jnp.float32),
                 pltpu.VMEM((1, rows), jnp.float32),
                 dma((3, heads)),
+                dma((3,)),
                 dma((3, kept)),
+                dma((3,)),
                 dma((3, kept)),
+                dma((3,)),
                 dma((3, kept)),
-                dma((3, kept)),
-                dma((3, kept)),
-                dma((3, kept)),
-                dma((2, 3, SHIPPED)),
+                dma((2, 3)),
                 dma((2, 3, SHIPPED)),
                 dma,
                 dma,
-                dma((heads,)),
             ],
             compiler_params=pltpu.CompilerParams(
                 collective_id=0, has_side_effects=True, vmem_limit_bytes=56 << 20
@@ -390,7 +396,15 @@
                 bytes_accessed=8 * rows * width,
                 transcendentals=4 * heads * rows * rows,
             ),
-        )(gain, queries, keys, values)
+        )(queries, keys, values)
+        return pl.pallas_call(
+            finish,
+            out_shape=jax.ShapeDtypeStruct(queries.shape, jnp.bfloat16),
+            in_specs=[whole] * 3,
+            out_specs=pl.BlockSpec(memory_space=pl.ANY),
+            scratch_shapes=[pltpu.VMEM((rows, width), jnp.bfloat16), dma((4,))],
+            compiler_params=pltpu.CompilerParams(vmem_limit_bytes=16 << 20),
+        )(gain, attended, scale)
 
     placed = (P("mp"), P("seq", "mp"), P("seq", "mp"), P("seq", "mp"))
     return jax.shard_map(

time: 101 us -> 95.5 us (0.946)
  local copies, waits for them, and re-layouts: 3.16 us -> 0.01 us
  Pallas kernels: 97.4 us -> 95.4 us
    pallas_call x1, Pallas kernels: 97.4 us -> 93.9 us  [shards(): pl.pallas_call(functools.partial(kernel, n, heads, kept, rows), out_shape...]
    unnamed x1 -> x2, local copies, waits for them, and re-layouts: 3.16 us -> 0.01 us
    pallas_call x0 -> x1, Pallas kernels: none -> 1.49 us  [shards(): pl.pallas_call(finish, out_shape=jax.ShapeDtypeStruct(queries.shape, jnp....]
where the time goes in v2:
time: 95.5 us; the launch traced here: 95.4 us
  Pallas kernels  95.4 us (100%)
    pallas_call x1, Pallas kernels, shards(): pl.pallas_call(functools.partial(kernel, n, heads, kept, rows), out_shape...  93.9 us

profile of v2, /device:TPU:24, one launch (start us, length us, event | category | flops | bytes accessed | tf_op | source)
XLA Modules:
  0.0 95.4 jit_solution(12186515035556992442)
XLA Ops:
  0.0 0.0 copy-start
  0.0 93.9 %shard_map.46 = (f32[16,512,128]{2,1,0:T(8,128)S(1)}, f32[512,128]{1,0:T(8,128)S(1)}) custom-call(bf16[512,2048]{1,0:T(8,128)(2,1)} %q_hbm.1, bf16[512,2048]{1,0:T(8,128)(2,1)} %k_hbm.1, bf16[512,2048]{1,0:T(8,128)(2,1)} %v_hbm.1), custom_call_target="tpu_custom_call" | custom-call | flops 8589934592 | bytes 8388608 | tf_op jit(solution)/shard_map/pallas_call | solution.py:355
  93.9 0.0 copy-done
  93.9 1.5 %shard_map.47 = bf16[512,2048]{1,0:T(8,128)(2,1)} custom-call(f32[16,1,128]{2,1,0:T(1,128)S(1)} %bitcast.1, f32[16,512,128]{2,1,0:T(8,128)S(1)} %get-tuple-element.7.attended, f32[512,128]{1,0:T(8,128)S(1)} %get-tuple-element.8.scale_ref), custom_call_target="tpu_custom_call" | custom-call | tf_op jit(solution)/shard_map/pallas_call | solution.py:400
Async XLA Ops:
  0.0 93.9 %copy-start = (f32[2048]{0:T(1024)S(1)}, f32[2048]{0:T(1024)}, u32[]{:S(2)}) copy-start(f32[2048]{0:T(1024)} %param.4) | copy-start | bytes 24580

commit v3 on v2

--- a/solution.py
+++ b/solution.py
@@ -15,9 +15,9 @@
 EXCLUDED = -1e30
 
 SHIPPED = 2
-LEAD = 2
-FORWARD_1, FORWARD_2, ATTEND, MERGE_2, MERGE_1, MERGE_0 = (1, 3), (1, 5), (4, 6), (6, 7), (7, 8), (10, 12)
-SHIP_1, SHIP_2, ATTEND_SHIPPED = (2, 2), (4, 5), (6, 7)
+LEAD = 1
+FORWARD_1, FORWARD_2, ATTEND, MERGE_2, MERGE_1, MERGE_0 = (2, 6), (2, 8), (5, 9), (7, 10), (9, 11), (15, 16)
+SHIP_1, SHIP_2, ATTEND_SHIPPED = (3, 6), (5, 8), (7, 10)
 SLOTS = max(b - a for a, b in zip(ATTEND, MERGE_0)) + 1
 TILE = 128
 
@@ -106,11 +106,6 @@
 
     pl.semaphore_signal(barrier, inc=1, device_id={"mp": partner}, device_id_type=MESH)
 
-    @pl.loop(0, heads)
-    def _(h):
-        for which in range(3):
-            load(which, h).start()
-
     squares[...] = jnp.zeros_like(squares)
 
     @pl.when(jnp.logical_not(has_left))
@@ -142,6 +137,11 @@
     def _():
         for h in range(min(LEAD, kept)):
             send_q(0, h).start()
+
+    @pl.loop(0, heads)
+    def _(h):
+        for which in range(3):
+            load(which, h).start()
 
     def rounds(skew):
         return skew[0] + lax.rem(me, 2) * (skew[1] - skew[0])
@@ -282,14 +282,14 @@
         staged_shipped(r, SHIP_2, functools.partial(ship, 2))
         staged_shipped(r, ATTEND_SHIPPED, attend_shipped)
         staged(r, FORWARD_1, 1, functools.partial(forward, 1))
-        staged(r, MERGE_0, 0, functools.partial(merge, 0))
-
-        @pl.when(has_left & (r + LEAD < kept))
-        def _():
-            send_q(0, r + LEAD).start()
-
         staged(r, MERGE_2, 2, functools.partial(merge, 2))
         staged(r, ATTEND, 0, attend)
+
+        @pl.when(has_left & (r + LEAD < kept))
+        def _():
+            send_q(0, r + LEAD).start()
+
+        staged(r, MERGE_0, 0, functools.partial(merge, 0))
         staged(r, FORWARD_2, 2, functools.partial(forward, 2))
         staged(r, MERGE_1, 1, functools.partial(merge, 1))
 

time: 95.5 us -> 95.3 us (level)
  no operation moved by 1% of the time
where the time goes in v3:
time: 95.3 us
  Pallas kernels  95.2 us (100%)
    pallas_call x1, Pallas kernels, shards(): pl.pallas_call(functools.partial(kernel, n, heads, kept, rows), out_shape...  93.8 us

profile of v3, /device:TPU:24, one launch (start us, length us, event | category | flops | bytes accessed | tf_op | source)
XLA Modules:
  0.0 95.3 jit_solution(18352206860753744823)
XLA Ops:
  0.0 0.0 copy-start
  0.0 93.8 %shard_map.46 = (f32[16,512,128]{2,1,0:T(8,128)S(1)}, f32[512,128]{1,0:T(8,128)S(1)}) custom-call(bf16[512,2048]{1,0:T(8,128)(2,1)} %q_hbm.1, bf16[512,2048]{1,0:T(8,128)(2,1)} %k_hbm.1, bf16[512,2048]{1,0:T(8,128)(2,1)} %v_hbm.1), custom_call_target="tpu_custom_call" | custom-call | flops 8589934592 | bytes 8388608 | tf_op jit(solution)/shard_map/pallas_call | solution.py:355
  93.8 0.0 copy-done
  93.8 1.5 %shard_map.47 = bf16[512,2048]{1,0:T(8,128)(2,1)} custom-call(f32[16,1,128]{2,1,0:T(1,128)S(1)} %bitcast.1, f32[16,512,128]{2,1,0:T(8,128)S(1)} %get-tuple-element.7.attended, f32[512,128]{1,0:T(8,128)S(1)} %get-tuple-element.8.scale_ref), custom_call_target="tpu_custom_call" | custom-call | tf_op jit(solution)/shard_map/pallas_call | solution.py:400
Async XLA Ops:
  0.0 93.8 %copy-start = (f32[2048]{0:T(1024)S(1)}, f32[2048]{0:T(1024)}, u32[]{:S(2)}) copy-start(f32[2048]{0:T(1024)} %param.4) | copy-start | bytes 24580

commit v4 on v2

--- a/solution.py
+++ b/solution.py
@@ -248,15 +248,14 @@
 
         @pl.when(me + 3 < n)
         def _():
+            send_l(0, h).start()
             send_o(0, h).start()
-            send_l(0, h).start()
 
     def merge(distance, h):
         step = 3 - distance
 
         @pl.when(has_left)
         def _():
-            send_o(step - 1, h).wait_recv()
             send_l(step - 1, h).wait_recv()
 
         slot = lax.rem(h, SLOTS)
@@ -265,13 +264,18 @@
         if distance:
             gap = -jnp.abs(here - before)
             l_out[step, h] = jnp.maximum(here, before) + jnp.log2(1.0 + jnp.exp2(gap))
+            send_l(step, h).start()
         share = row_to_lanes(share)
+
+        @pl.when(has_left)
+        def _():
+            send_o(step - 1, h).wait_recv()
+
         mine = o_own[slot, distance]
         mixed = mine + share * (o_in[step - 1, h].astype(jnp.float32) - mine)
         if distance:
             o_out[step, h] = mixed.astype(jnp.bfloat16)
             send_o(step, h).start()
-            send_l(step, h).start()
         else:
             attended[h] = mixed
             squares[...] += mixed * mixed

time: 95.5 us -> 95.4 us (level)
  no operation moved by 1% of the time
where the time goes in v4:
time: 95.4 us
  Pallas kernels  95.3 us (100%)
    pallas_call x1, Pallas kernels, shards(): pl.pallas_call(functools.partial(kernel, n, heads, kept, rows), out_shape...  93.9 us

profile of v4, /device:TPU:24, one launch (start us, length us, event | category | flops | bytes accessed | tf_op | source)
XLA Modules:
  0.0 95.4 jit_solution(18053074666930109527)
XLA Ops:
  0.0 0.0 copy-start
  0.0 93.9 %shard_map.46 = (f32[16,512,128]{2,1,0:T(8,128)S(1)}, f32[512,128]{1,0:T(8,128)S(1)}) custom-call(bf16[512,2048]{1,0:T(8,128)(2,1)} %q_hbm.1, bf16[512,2048]{1,0:T(8,128)(2,1)} %k_hbm.1, bf16[512,2048]{1,0:T(8,128)(2,1)} %v_hbm.1), custom_call_target="tpu_custom_call" | custom-call | flops 8589934592 | bytes 8388608 | tf_op jit(solution)/shard_map/pallas_call | solution.py:359
  93.9 0.0 copy-done
  93.9 1.5 %shard_map.47 = bf16[512,2048]{1,0:T(8,128)(2,1)} custom-call(f32[16,1,128]{2,1,0:T(1,128)S(1)} %bitcast.1, f32[16,512,128]{2,1,0:T(8,128)S(1)} %get-tuple-element.7.attended, f32[512,128]{1,0:T(8,128)S(1)} %get-tuple-element.8.scale_ref), custom_call_target="tpu_custom_call" | custom-call | tf_op jit(solution)/shard_map/pallas_call | solution.py:404
Async XLA Ops:
  0.0 93.9 %copy-start = (f32[2048]{0:T(1024)S(1)}, f32[2048]{0:T(1024)}, u32[]{:S(2)}) copy-start(f32[2048]{0:T(1024)} %param.4) | copy-start | bytes 24580
